TPU v7x, 128 devices: a whole 4x4x4 slice. The times are simulated.
128 devices in a mesh: expert: 16 (over x, y), row: 8 (over z, core).
Axes of the slice: x: 4, y: 4, z: 4, core: 2. Of those that a mesh axis runs over, the one named last changes fastest.
Arguments:
- weights: bfloat16 [64, 7168, 2048], P('expert', 'row'), may hold values from -0.0625 to 0.0625
- prev_rows: float32 [7168, 512], P('row'), may hold values from -6 to 6
- prev_cols: float32 [2048, 256], replicated, may hold values from -6 to 6
Outputs:
- row_basis: float32 [7168, 512], P('row')
- col_basis: float32 [2048, 256], replicated
All inputs are finite; a program needn't handle non-finite values.
Results may differ from a plain program's by a relative error of at most 0.004.
Values sent between devices are 32-bit elements; how exact they have to be, the bound alone decides.
A program may use at most 128 MiB of HBM per device.

v0:
```python
import math

import jax
import jax.numpy as jnp
from jax import lax
from jax.sharding import PartitionSpec as P

D = 7168
F = 2048


def orthogonal_part(images, gram, scale):
    factor = jnp.linalg.cholesky(gram)
    return scale * jax.scipy.linalg.solve_triangular(factor, images.T, lower=True).T


def cores_under(row_basis, proj):
    partial_two = jnp.einsum("rj,erk->ejk", row_basis, proj, precision=lax.Precision.HIGHEST)
    return lax.psum(partial_two, "row")


def shards(weights, prev_rows, prev_cols):
    highest = lax.Precision.HIGHEST
    cols_low = prev_cols.astype(jnp.bfloat16)
    proj = jnp.einsum("erf,fk->erk", weights, cols_low, preferred_element_type=jnp.float32)
    partial_cores = jnp.einsum("rj,erk->ejk", prev_rows, proj, precision=highest)
    cores = lax.psum(partial_cores, "row")
    local_images = jnp.einsum("erk,ejk->rj", proj, cores, precision=highest)
    images = lax.psum(local_images, "expert")
    row_gram = lax.psum(jnp.dot(images.T, images, precision=highest), "row")
    row_basis = orthogonal_part(images, row_gram, math.sqrt(D))
    cores_two = cores_under(row_basis, proj)
    back = jnp.einsum("rj,ejk->erk", row_basis, cores_two, precision=highest).astype(jnp.bfloat16)
    terms = jnp.einsum("erf,erk->fk", weights, back, preferred_element_type=jnp.float32)
    colimg = lax.psum(terms, ("expert", "row"))
    col_gram = jnp.dot(colimg.T, colimg, precision=highest)
    col_basis = orthogonal_part(colimg, col_gram, math.sqrt(F))
    return (row_basis, col_basis)


def solution(mesh):
    placed = (P("expert", "row", None), P("row", None), P())
    return jax.shard_map(
        shards, mesh=mesh, in_specs=placed, out_specs=(P("row", None), P()), check_vma=False
    )
```

profile of v0, /device:TPU:1, one launch (start us, length us, event | category | flops | bytes accessed | tf_op | source)
XLA Modules:
  0.0 748.0 jit_solution(15499366686109663881)
XLA Ops:
  7.2 8.2 %fusion.28 = f32[4,896,256]{2,1,0:T(8,128)S(1)} fusion(bf16[4,896,2048]{2,1,0:T(8,128)(2,1)} %param.5, f32[2048,256]{1,0:T(8,128)} %param.7), kind=kOutput, calls=%fused_computation.42 | convolution fusion | flops 3758620672 | bytes 20447232 | tf_op jit(solution)/shard_map/erf,fk->erk/dot_general | solution.py:25
  17.2 8.2 %fusion.9 = f32[4,512,256]{2,1,0:T(8,128)} fusion(f32[4,896,256]{2,1,0:T(8,128)S(1)} %fusion.28, f32[896,512]{1,0:T(8,128)S(1)} %copy-done), kind=kOutput, calls=%fused_computation.17 | convolution fusion | flops 5637144576 | bytes 7602176 | tf_op jit(solution)/shard_map/rj,erk->ejk/dot_general | solution.py:26
  25.6 67.1 %all-reduce.8.cloned.1.call-done = f32[4,512,256]{2,1,0:T(8,128)} async-done(((f32[4,512,256]{2,1,0:T(8,128)}), f32[4,512,256]{2,1,0:T(8,128)}) %all-reduce.8.cloned.1.call-update) | async-done | bytes 2097168 | tf_op jit(solution)/shard_map/psum | solution.py:27
  92.8 9.3 %convolution_bitcast_fusion.1 = f32[896,512]{1,0:T(8,128)} fusion(f32[4,896,256]{2,1,0:T(8,128)} %copy-done.1, f32[4,512,256]{2,1,0:T(8,128)} %all-reduce.8.cloned.1.call-done), kind=kOutput, calls=%fused_computation.19 | convolution fusion | flops 5637144576 | bytes 7602176 | tf_op jit(solution)/shard_map/erk,ejk->rj/dot_general | solution.py:28
  102.2 89.3 %all-reduce.10.cloned.1.call-done = f32[896,512]{1,0:T(8,128)} async-done(((f32[896,512]{1,0:T(8,128)}), f32[896,512]{1,0:T(8,128)}) %all-reduce.10.cloned.1.call-update) | async-done | bytes 1835024 | tf_op jit(solution)/shard_map/psum | solution.py:29
  198.5 61.1 %all-reduce.12.cloned.1.call-done = f32[512,512]{0,1:T(8,128)} async-done(((f32[512,512]{0,1:T(8,128)}), f32[512,512]{0,1:T(8,128)}) %all-reduce.12.cloned.1.call-update) | async-done | bytes 1048592 | tf_op jit(solution)/shard_map/psum | solution.py:30
  264.6 11.7 %cholesky.135 = f32[128,128]{1,0:T(8,128)S(1)} custom-call(f32[128,128]{1,0:T(8,128)S(1)} %cholesky.339), custom_call_target="Cholesky" | custom-call | tf_op jit(solution)/shard_map/jit(cholesky)/cholesky | solution.py:13
  276.4 9.8 %custom-call.39 = f32[1,128,128]{1,2,0:T(8,128)S(1)} custom-call(f32[1,128,128]{2,1,0:T(8,128)S(1)} %get-tuple-element.54), custom_call_target="InvertDiagBlocksLowerTriangular" | custom-call | tf_op jit(solution)/shard_map/jit(cholesky)/cholesky | solution.py:13
  288.9 11.7 %cholesky.158 = f32[128,128]{1,0:T(8,128)S(1)} custom-call(f32[128,128]{1,0:T(8,128)S(1)} %cholesky.343), custom_call_target="Cholesky" | custom-call | tf_op jit(solution)/shard_map/jit(cholesky)/cholesky | solution.py:13
  300.6 10.0 %custom-call.40 = f32[1,128,128]{1,2,0:T(8,128)S(1)} custom-call(f32[1,128,128]{2,1,0:T(8,128)S(1)} %get-tuple-element.51), custom_call_target="InvertDiagBlocksLowerTriangular" | custom-call | tf_op jit(solution)/shard_map/jit(cholesky)/cholesky | solution.py:13
  312.1 11.7 %cholesky.292 = f32[128,128]{1,0:T(8,128)S(1)} custom-call(f32[128,128]{1,0:T(8,128)S(1)} %cholesky.348), custom_call_target="Cholesky" | custom-call | tf_op jit(solution)/shard_map/jit(cholesky)/cholesky | solution.py:13
  324.5 9.8 %custom-call.44 = f32[1,128,128]{1,2,0:T(8,128)S(1)} custom-call(f32[1,128,128]{2,1,0:T(8,128)S(1)} %get-tuple-element.48), custom_call_target="InvertDiagBlocksLowerTriangular" | custom-call | tf_op jit(solution)/shard_map/jit(cholesky)/cholesky/custom-call.10 | solution.py:13
  335.8 11.7 %cholesky.305 = f32[128,128]{1,0:T(8,128)S(1)} custom-call(f32[128,128]{1,0:T(8,128)S(1)} %convolution_subtract_fusion.6), custom_call_target="Cholesky" | custom-call | tf_op jit(solution)/shard_map/jit(cholesky)/cholesky | solution.py:13
  352.8 14.0 %while.2 = (s32[]{:T(128)}, f32[512,512]{1,0:T(8,128)}, s32[4,2]{0,1:T(2,128)S(1)}, f32[4,128,128]{2,1,0:T(8,128)}, s32[]{:T(128)}) while((s32[]{:T(128)}, f32[512,512]{1,0:T(8,128)}, s32[4,2]{0,1:T(2,128)S(1)}, f32[4,128,128]{2,1,0:T(8,128)}, s32[]{:T(128)}) %tuple.50), condition=%wide.while_cond, body=%wide.while_body.sunk | while | flops 2 | bytes 132705 | solution.py:14
  366.8 40.1 %custom-call.41 = f32[4,128,128]{1,2,0:T(8,128)S(1)} custom-call(f32[4,128,128]{2,1,0:T(8,128)} %get-tuple-element.10), custom_call_target="InvertDiagBlocksLowerTriangular" | custom-call | tf_op jit(solution)/shard_map/jit(_solve_triangular)/triangular_solve | solution.py:14
  419.5 13.4 %fusion.12 = f32[4,512,256]{1,2,0:T(8,128)} fusion(f32[4,896,256]{2,1,0:T(8,128)S(1)} %copy-done.2, f32[128,896]{1,0:T(8,128)S(1)} %fusion.49, f32[128,896]{1,0:T(8,128)S(1)} %fusion.50, f32[128,896]{1,0:T(8,128)S(1)} %fusion.52, f32[128,896]{1,0:T(8,128)S(1)} %fusion.34), kind=kOutput, calls=%fused_computation.18 | convolution fusion | flops 5638979584 | bytes 7602176 | tf_op jit(solution)/shard_map/rj,erk->ejk/dot_general | solution.py:18
  433.0 65.4 %all-reduce.14.cloned.1.call-done = f32[4,512,256]{1,2,0:T(8,128)} async-done(((f32[4,512,256]{1,2,0:T(8,128)}), f32[4,512,256]{1,2,0:T(8,128)}) %all-reduce.14.cloned.1.call-update) | async-done | bytes 2097168 | tf_op jit(solution)/shard_map/psum | solution.py:19
  498.4 8.5 %fusion.2 = bf16[4,256,896]{2,1,0:T(8,128)(2,1)S(1)} fusion(f32[4,512,256]{1,2,0:T(8,128)} %all-reduce.14.cloned.1.call-done, f32[128,896]{1,0:T(8,128)} %copy-done.6, f32[128,896]{1,0:T(8,128)S(1)} %fusion.50, f32[128,896]{1,0:T(8,128)S(1)} %fusion.52, f32[128,896]{1,0:T(8,128)S(1)} %fusion.34), kind=kOutput, calls=%fused_computation.10 | convolution fusion | flops 5638979584 | bytes 5767168 | tf_op jit(solution)/shard_map/rj,ejk->erk/dot_general | solution.py:33
  506.8 8.8 %convolution_bitcast_fusion = f32[2048,256]{0,1:T(8,128)} fusion(bf16[4,896,2048]{2,1,0:T(8,128)(2,1)} %param.5, bf16[4,256,896]{2,1,0:T(8,128)(2,1)S(1)} %fusion.2), kind=kOutput, calls=%fused_computation.4 | convolution fusion | flops 3758096384 | bytes 18612224 | tf_op jit(solution)/shard_map/erf,erk->fk/dot_general | solution.py:34
  521.0 146.5 %all-reduce.16.cloned.1.call-done = f32[2048,256]{0,1:T(8,128)} async-done(((f32[2048,256]{0,1:T(8,128)}), f32[2048,256]{0,1:T(8,128)}) %all-reduce.16.cloned.1.call-update) | async-done | bytes 2097168 | tf_op jit(solution)/shard_map/psum | solution.py:35
  671.7 11.7 %cholesky.317 = f32[128,128]{1,0:T(8,128)S(1)} custom-call(f32[128,128]{1,0:T(8,128)S(1)} %cholesky.352), custom_call_target="Cholesky" | custom-call | tf_op jit(solution)/shard_map/jit(cholesky)/cholesky | solution.py:13
  683.5 9.8 %custom-call.45 = f32[1,128,128]{1,2,0:T(8,128)S(1)} custom-call(f32[1,128,128]{2,1,0:T(8,128)S(1)} %get-tuple-element.44), custom_call_target="InvertDiagBlocksLowerTriangular" | custom-call | tf_op jit(solution)/shard_map/jit(cholesky)/cholesky/custom-call.10 | solution.py:13
  693.8 11.7 %cholesky.326 = f32[128,128]{1,0:T(8,128)S(1)} custom-call(f32[128,128]{1,0:T(8,128)S(1)} %convolution_subtract_fusion.5), custom_call_target="Cholesky" | custom-call | tf_op jit(solution)/shard_map/jit(cholesky)/cholesky | solution.py:13
  712.4 19.7 %custom-call.42 = f32[2,128,128]{1,2,0:T(8,128)S(1)} custom-call(f32[2,128,128]{2,1,0:T(8,128)S(1)} %get-tuple-element.18), custom_call_target="InvertDiagBlocksLowerTriangular" | custom-call | tf_op jit(solution)/shard_map/jit(_solve_triangular)/triangular_solve | solution.py:14
  (98 shorter events, 78.4 us)
Async XLA Ops:
  7.2 10.0 %copy-start = (f32[896,512]{1,0:T(8,128)S(1)}, f32[896,512]{1,0:T(8,128)}, u32[]{:S(2)}) copy-start(f32[896,512]{1,0:T(8,128)} %param.6) | copy-start | bytes 5505028
  7.2 85.6 %all-reduce.8.cloned.1.call-start = ((), (), s32[]{:S(2)}) async-start(), calls=%async_computation | async-start | bytes 4194304 | tf_op jit(solution)/shard_map/psum | solution.py:27
  15.4 1.8 copy-start.1
  25.4 166.1 %all-reduce.10.cloned.1.call-start = ((), (), s32[]{:S(2)}) async-start(), calls=%async_computation.1 | async-start | bytes 3670016 | tf_op jit(solution)/shard_map/psum | solution.py:29
  102.1 157.5 %all-reduce.12.cloned.1.call-start = ((), (), s32[]{:S(2)}) async-start(), calls=%async_computation.2 | async-start | bytes 2097152 | tf_op jit(solution)/shard_map/psum | solution.py:30
  198.0 300.4 %all-reduce.14.cloned.1.call-start = ((), (), s32[]{:S(2)}) async-start(), calls=%async_computation.3 | async-start | bytes 4194304 | tf_op jit(solution)/shard_map/psum | solution.py:19
  259.6 2.6 copy-start.5
  263.7 1.0 copy-start.7
  406.9 4.4 copy-start.4
  413.8 5.7 copy-start.2
  418.7 0.8 copy-start.6
  432.9 234.5 %all-reduce.16.cloned.1.call-start = ((), (), s32[]{:S(2)}) async-start(), calls=%async_computation.4 | async-start | bytes 4194304 | tf_op jit(solution)/shard_map/psum | solution.py:35
  732.1 2.4 copy-start.3
Sparse Core Ops, SparseCore 0:
  25.5 67.2 all-reduce.7
  102.2 89.1 all-reduce.9
  198.1 61.4 all-reduce.11
  433.0 65.2 all-reduce.13
  515.7 151.6 all-reduce.15
where the time goes:
time: 756 us; the launch traced here: 748 us
  waiting for transfers between devices  429 us (57%)
  other arithmetic  180 us (24%)
  matrix products  89 us (12%)
  local copies, waits for them, and re-layouts  30.2 us (4%)
  between operations  18.4 us (2%)
    psum x1, waiting for transfers between devices, shards(): colimg = lax.psum(terms, ('expert', 'row'))  146 us
    another operation x21, other arithmetic, orthogonal_part(): factor = jnp.linalg.cholesky(gram)  113 us
    psum x1, waiting for transfers between devices, shards(): images = lax.psum(local_images, 'expert')  89.3 us
    psum x1, waiting for transfers between devices, shards(): cores = lax.psum(partial_cores, 'row')  67.1 us
    psum x1, waiting for transfers between devices, cores_under(): return lax.psum(partial_two, 'row')  65.4 us
    another operation x6, other arithmetic, orthogonal_part(): jax.scipy.linalg.solve_triangular(factor, images.T, lower=True)  61.3 us
    psum x1, waiting for transfers between devices, shards(): row_gram = lax.psum(jnp.dot(images.T, images, precision=highest), 'row')  61.1 us
    another operation x18, local copies, waits for them, and re-layouts  17.9 us
  transfers between devices with their start and end apart: 5, of which 5 were waited for; matrix products, arithmetic and copies ran while one was open for 1% of the time, Pallas kernels for 0%

commit v1 on v0

v1 whole, which is shorter than its diff:
```python
import functools
import math

import jax
import jax.numpy as jnp
from jax import lax
from jax.experimental import pallas as pl
from jax.experimental.pallas import tpu as pltpu
from jax.sharding import PartitionSpec as P

D = 7168
F = 2048
R1 = 512
R2 = 256
ROWS = 896
LOCAL = 4
MESH = pl.DeviceIdType.MESH
HIGHEST = lax.Precision.HIGHEST
F32 = jnp.float32
BF16 = jnp.bfloat16


def dot(a, b, ca, cb, precision=None):
    return lax.dot_general(
        a, b, (((ca,), (cb,)), ((), ())), precision=precision, preferred_element_type=F32
    )


def split(value):
    high = value.astype(BF16)
    return high, (value - high.astype(F32)).astype(BF16)


def dot3(ah, al, bh, bl, ca, cb):
    return dot(ah, bh, ca, cb) + (dot(ah, bl, ca, cb) + dot(al, bh, ca, cb))


def lane_of(block, j):
    return jnp.broadcast_to(block[:, j : j + 1], (8, 128))


def row_of(block, k):
    return jnp.broadcast_to(block[k : k + 1, :], (8, 128))


def inverse_factor_of_tile(blocks):
    count = 16
    sub = lax.broadcasted_iota(jnp.int32, (8, 128), 0)
    lane = lax.broadcasted_iota(jnp.int32, (8, 128), 1)
    left = list(blocks)
    right = [jnp.where(lane == sub + 8 * b, 1.0, 0.0).astype(F32) for b in range(count)]
    for b in range(count):
        columns = [lane_of(left[b], 8 * b + j) for j in range(8)]
        corner = {(k, j): row_of(columns[j], k) for j in range(8) for k in range(j, 8)}
        last = b == count - 1
        lrows = None if last else [row_of(left[b], k) for k in range(8)]
        rrows = [row_of(right[b], k) for k in range(8)]
        roots, low = [], {}
        for i in range(8):
            root = lax.rsqrt(corner[i, i])
            roots.append(root)
            for k in range(i + 1, 8):
                low[k, i] = corner[k, i] * root
            for j in range(i + 1, 8):
                for k in range(j, 8):
                    corner[k, j] = corner[k, j] - low[k, i] * low[j, i]
            rrows[i] = rrows[i] * root
            for k in range(i + 1, 8):
                rrows[k] = rrows[k] - low[k, i] * rrows[i]
            if not last:
                lrows[i] = lrows[i] * root
                for k in range(i + 1, 8):
                    lrows[k] = lrows[k] - low[k, i] * lrows[i]
        whole = rrows[7]
        for i in range(6, -1, -1):
            whole = jnp.where(sub == i, rrows[i], whole)
        right[b] = whole
        for t in range(b + 1, count):
            q = [lane_of(left[t], 8 * b + j) for j in range(8)]
            lt, rt = left[t], right[t]
            for i in range(8):
                term = q[i] * roots[i]
                for k in range(i + 1, 8):
                    q[k] = q[k] - low[k, i] * term
                lt = lt - term * lrows[i]
                rt = rt - term * rrows[i]
            left[t], right[t] = lt, rt
    return right


def inverse_factor(n, gram, inverse, between=None):
    tiles = n // 128
    inverse[...] = jnp.zeros_like(inverse)

    def step(k, carry):
        o = pl.multiple_of(k * 128, 128)
        rows = inverse_factor_of_tile(
            [gram[pl.ds(o + 8 * b, 8), pl.ds(o, 128)] for b in range(16)]
        )
        inverse[pl.ds(o, 128), pl.ds(o, 128)] = jnp.concatenate(rows, axis=0)
        for kk in range(tiles):

            @pl.when(k == kk)
            def _():
                a, z = 128 * kk, 128 * kk + 128
                own = inverse[a:z, a:z]
                if kk > 0:
                    inverse[a:z, 0:a] = dot(own, inverse[a:z, 0:a], 1, 0, HIGHEST)
                if kk < tiles - 1:
                    upper = dot(own, gram[a:z, z:n], 1, 0, HIGHEST)
                    gram[z:n, z:n] = gram[z:n, z:n] - dot(upper, upper, 0, 0, HIGHEST)
                    inverse[z:n, 0:z] = inverse[z:n, 0:z] - dot(
                        upper, inverse[a:z, 0:z], 0, 0, HIGHEST
                    )
                if between is not None:
                    between(kk)

        return carry

    lax.fori_loop(0, tiles, step, 0)


class Place:
    def __init__(self):
        expert, row = lax.axis_index("expert"), lax.axis_index("row")
        self.at = {
            "x": lax.div(expert, 4), "y": lax.rem(expert, 4),
            "z": lax.div(row, 2), "c": lax.rem(row, 2),
        }

    def index(self, axis, d):
        return lax.rem(self.at[axis] + d, 4)

    def peer(self, axis, d):
        at = dict(self.at)
        at[axis] = lax.rem(at[axis] + d, 2 if axis == "c" else 4)
        return (at["x"] * 4 + at["y"], at["z"] * 2 + at["c"])


class Sender:
    def __init__(self, place, send_sem, recv_sem):
        self.place, self.send_sem, self.recv_sem, self.used = place, send_sem, recv_sem, 0

    def copy(self, source, target, axis, d):
        n = self.used
        self.used += 1
        return pltpu.make_async_remote_copy(
            src_ref=source, dst_ref=target, send_sem=self.send_sem.at[n],
            recv_sem=self.recv_sem.at[n], device_id=self.place.peer(axis, d), device_id_type=MESH,
        )


class RowSum:
    def __init__(self, sender, rows, part, sibling, arrived, full):
        place = sender.place
        c = place.at["c"]
        half, chunk = rows // 2, rows // 8
        self.half, self.chunk, self.c = half, chunk, c
        self.part, self.sibling, self.arrived, self.full = part, sibling, arrived, full
        self.base = c * half
        other = (1 - c) * half
        self.place = place
        self.swap = sender.copy(part.at[pl.ds(other, half)], sibling, "c", 1)
        self.spread = [
            sender.copy(
                part.at[pl.ds(self.base + place.index("z", d) * chunk, chunk)],
                arrived.at[d - 1], "z", d,
            )
            for d in (1, 2, 3)
        ]
        self.mine = self.base + place.at["z"] * chunk
        own = full.at[pl.ds(self.mine, chunk)]
        self.gather = [sender.copy(own, own, "z", d) for d in (1, 2, 3)]
        self.across = [sender.copy(own, own, "c", 1)]
        for d in (1, 2, 3):
            got = full.at[pl.ds(self.base + place.index("z", 4 - d) * chunk, chunk)]
            self.across.append(sender.copy(got, got, "c", 1))

    def start(self):
        self.swap.start()

    def scatter(self):
        self.swap.wait_recv()
        for d in (1, 2, 3, 0):
            p = self.place.index("z", d)
            there = pl.ds(self.base + p * self.chunk, self.chunk)
            self.part[there] = self.part[there] + self.sibling[pl.ds(p * self.chunk, self.chunk)]
            if d:
                self.spread[d - 1].start()

    def reduce(self):
        for copy in self.spread:
            copy.wait_recv()
        there = pl.ds(self.mine, self.chunk)
        self.full[there] = (self.part[there] + self.arrived[0]) + (
            self.arrived[1] + self.arrived[2]
        )
        for copy in self.gather:
            copy.start()
        self.across[0].start()

    def forward(self):
        for d in (1, 2, 3):
            self.gather[d - 1].wait_recv()
            self.across[d].start()

    def finish(self):
        for copy in self.across:
            copy.wait()
        self.swap.wait_send()
        for copy in self.spread + self.gather:
            copy.wait_send()


class PlaneSum:
    def __init__(self, sender, first, second, part, arrived1, half, arrived2, full):
        place = sender.place
        m1, m2 = place.at[first], place.at[second]
        self.part, self.arrived1, self.half = part, arrived1, half
        self.arrived2, self.full, self.m1, self.m2 = arrived2, full, m1, m2
        self.one = [
            sender.copy(
                part.at[pl.ds(place.index(first, d) * 224, 224)], arrived1.at[d - 1], first, d
            )
            for d in (1, 2, 3)
        ]
        self.two = [
            sender.copy(
                half.at[pl.ds(place.index(second, d) * 56, 56)], arrived2.at[d - 1], second, d
            )
            for d in (1, 2, 3)
        ]
        own = full.at[pl.ds(m1 * 224 + m2 * 56, 56)]
        self.three = [sender.copy(own, own, second, d) for d in (1, 2, 3)]
        wide = full.at[pl.ds(m1 * 224, 224)]
        self.four = [sender.copy(wide, wide, first, d) for d in (1, 2, 3)]

    def start(self):
        for copy in self.one:
            copy.start()

    def reduce1(self):
        for copy in self.one:
            copy.wait_recv()
        a = self.arrived1
        self.half[...] = (self.part[pl.ds(self.m1 * 224, 224)] + a[0]) + (a[1] + a[2])
        for copy in self.two:
            copy.start()

    def reduce2(self):
        for copy in self.two:
            copy.wait_recv()
        a = self.arrived2
        self.full[pl.ds(self.m1 * 224 + self.m2 * 56, 56)] = (
            self.half[pl.ds(self.m2 * 56, 56)] + a[0]
        ) + (a[1] + a[2])
        for copy in self.three:
            copy.start()

    def gather(self):
        for copy in self.three:
            copy.wait_recv()
        for copy in self.four:
            copy.start()

    def finish(self):
        for copy in self.four:
            copy.wait_recv()
        for copy in self.one + self.two + self.three + self.four:
            copy.wait_send()


class CubeSum:
    def __init__(self, sender, axes, u0, n, part, arrived1, sum1, arrived2, sum2, arrived3, full):
        place = sender.place
        a1, a2, a3 = axes
        m1, m2, m3 = (place.at[a] for a in axes)
        base = place.at["c"] * 8 + u0
        slabs = pl.ds(u0, n)
        self.slabs, self.m1, self.m2, self.m3, self.base, self.n = slabs, m1, m2, m3, base, n
        self.part, self.arrived1, self.sum1 = part, arrived1, sum1
        self.arrived2, self.sum2, self.arrived3, self.full = arrived2, sum2, arrived3, full
        self.one = [
            sender.copy(
                part.at[pl.ds(base, n), pl.ds(place.index(a1, d) * 64, 64)],
                arrived1.at[d - 1, slabs], a1, d,
            )
            for d in (1, 2, 3)
        ]
        self.two = [
            sender.copy(
                sum1.at[slabs, pl.ds(place.index(a2, d) * 16, 16)],
                arrived2.at[d - 1, slabs], a2, d,
            )
            for d in (1, 2, 3)
        ]
        self.three = [
            sender.copy(arrived3.at[m3, slabs], arrived3.at[m3, slabs], a3, d) for d in (1, 2, 3)
        ]
        own = full.at[pl.ds(base, n), pl.ds(m1 * 64 + m2 * 16, 16)]
        self.four = [sender.copy(own, own, a2, d) for d in (1, 2, 3)]
        wide = full.at[pl.ds(base, n), pl.ds(m1 * 64, 64)]
        self.five = [sender.copy(wide, wide, a1, d) for d in (1, 2, 3)]
        whole = full.at[pl.ds(base, n)]
        self.six = sender.copy(whole, whole, "c", 1)

    def start(self):
        for copy in self.one:
            copy.start()

    def reduce1(self):
        for copy in self.one:
            copy.wait_recv()
        a, s = self.arrived1, self.slabs
        own = self.part[pl.ds(self.base, self.n), pl.ds(self.m1 * 64, 64)]
        self.sum1[s] = (own + a[0, s]) + (a[1, s] + a[2, s])
        for copy in self.two:
            copy.start()

    def reduce2(self):
        for copy in self.two:
            copy.wait_recv()
        a, s = self.arrived2, self.slabs
        own = self.sum1[s, pl.ds(self.m2 * 16, 16)]
        self.arrived3[self.m3, s] = (own + a[0, s]) + (a[1, s] + a[2, s])
        for copy in self.three:
            copy.start()

    def reduce3(self):
        for copy in self.three:
            copy.wait()
        a, s = self.arrived3, self.slabs
        self.full[pl.ds(self.base, self.n), pl.ds(self.m1 * 64 + self.m2 * 16, 16)] = (
            a[0, s] + a[1, s]
        ) + (a[2, s] + a[3, s])
        for copy in self.four:
            copy.start()

    def gather(self):
        for copy in self.four:
            copy.wait_recv()
        for copy in self.five:
            copy.start()

    def across(self):
        for copy in self.five:
            copy.wait_recv()
        self.six.start()

    def finish(self):
        self.six.wait()
        for copy in self.one + self.two + self.four + self.five:
            copy.wait_send()


def kernel(
    w_hbm, x_hbm, c_hbm, rb_hbm, cb_hbm,
    w, ph, pw, pth, ptw, xh, xw, cols, pf,
    cp, csib, carr, cfull, ch, cw,
    ip, iarr1, ihalf, iarr2, imf,
    gp, gsib, garr, gfull, gram, inv, vh, vw, th, tw,
    rb, dp, dsib, darr1, dsum1, darr2, dsum2, darr3, df,
    local_sem, send_sem, recv_sem,
):
    place = Place()
    c = place.at["c"]
    loads = [
        pltpu.make_async_copy(
            c_hbm.at[pl.ds(256 * t, 256), pl.ds(128 * s, 128)], df.at[8 * s + t],
            local_sem.at[11 + 8 * s + t],
        )
        for s in range(2)
        for t in range(8)
    ]
    order = [lax.rem(2 * (1 - c) + s, 4) for s in range(4)]
    wloads = [
        pltpu.make_async_copy(w_hbm.at[order[s]], w.at[order[s]], local_sem.at[2 + s])
        for s in range(4)
    ]
    xloads = [
        pltpu.make_async_copy(x_hbm.at[:, pl.ds(128 * q, 128)], imf.at[q], local_sem.at[6 + q])
        for q in range(4)
    ]
    for load in loads + wloads[:1] + xloads + wloads[1:]:
        load.start()

    barrier = pltpu.get_barrier_semaphore()
    pl.semaphore_signal(barrier, inc=1, device_id=place.peer("c", 1), device_id_type=MESH)
    for axis in ("x", "y", "z"):
        for d in (1, 2, 3):
            pl.semaphore_signal(barrier, inc=1, device_id=place.peer(axis, d), device_id_type=MESH)

    sender = Sender(place, send_sem, recv_sem)

    for n, load in enumerate(loads):
        load.wait()
        s, t = n // 8, n % 8
        cols[256 * t : 256 * t + 256, 128 * s : 128 * s + 128] = df[n].astype(BF16)
    for q, load in enumerate(xloads):
        load.wait()
        h, lo = split(imf[q])
        xh[:, 128 * q : 128 * q + 128] = h
        xw[:, 128 * q : 128 * q + 128] = lo

    cores = [
        RowSum(sender, 1024, cp.at[j], csib.at[j], carr.at[j], cfull.at[j]) for j in range(2)
    ]
    for s in range(4):
        e = order[s]
        wloads[s].wait()
        at = pl.ds(pl.multiple_of(e * 256, 256), 256)

        def project(i, carry, e=e, at=at):
            r = pl.ds(pl.multiple_of(i * 224, 32), 224)
            value = dot(w[e, r, :], cols[...], 1, 0)
            pf[r, :] = value
            h, lo = split(value)
            ph[r, at] = h
            pw[r, at] = lo
            return carry

        lax.fori_loop(0, 4, project, 0)
        h, lo = split(pf[...].T)
        pth[at, :] = h
        ptw[at, :] = lo
        value = dot3(pth[at, :], ptw[at, :], xh[...], xw[...], 1, 0)
        cp[0, at, :] = value[:, :256]
        cp[1, at, :] = value[:, 256:]
        if s == 1:
            pl.semaphore_wait(barrier, 10)
            for one in cores:
                one.start()
    for one in cores:
        one.scatter()
    for one in cores:
        one.reduce()

    planes = [
        PlaneSum(
            sender, "xy"[q % 2], "yx"[q % 2], ip.at[q], iarr1.at[q], ihalf.at[q], iarr2.at[q],
            imf.at[q],
        )
        for q in range(4)
    ]
    for j in range(2):
        cores[j].forward()
        cores[j].finish()
        h, lo = split(cfull[j])
        ch[...] = h
        cw[...] = lo

        def image(i, carry, j=j):
            r = pl.ds(pl.multiple_of(i * 224, 32), 224)
            value = dot3(ph[r, :], pw[r, :], ch[...], cw[...], 1, 0)
            ip[2 * j, r, :] = value[:, :128]
            ip[2 * j + 1, r, :] = value[:, 128:]
            return carry

        lax.fori_loop(0, 4, image, 0)
        planes[2 * j].start()
        planes[2 * j + 1].start()
    for one in planes:
        one.reduce1()
    for one in planes:
        one.reduce2()
    for one in planes:
        one.gather()

    def gram_part(i, j):
        a, b = slice(256 * i, 256 * i + 256), slice(256 * j, 256 * j + 256)
        return dot3(xh[:, a], xw[:, a], xh[:, b], xw[:, b], 0, 0)

    for q in range(4):
        planes[q].finish()
        h, lo = split(imf[q])
        xh[:, 128 * q : 128 * q + 128] = h
        xw[:, 128 * q : 128 * q + 128] = lo
        if q == 1:
            gp[0:256] = gram_part(0, 0)
    gp[256:512] = gram_part(0, 1)
    gp[512:768] = gram_part(1, 1)
    grams = RowSum(sender, 768, gp, gsib, garr, gfull)
    grams.start()
    backs = [
        RowSum(sender, 1024, cp.at[j], csib.at[j], carr.at[j], cfull.at[j]) for j in range(2)
    ]

    def under(j):
        def body(i, carry):
            r = pl.ds(pl.multiple_of(i * 256, 256), 256)
            a = slice(256 * j, 256 * j + 256)
            cp[j, r, :] = dot3(pth[r, :], ptw[r, :], xh[:, a], xw[:, a], 1, 0)
            return carry

        lax.fori_loop(0, 4, body, 0)

    grams.scatter()
    under(0)
    grams.reduce()
    under(1)
    grams.forward()
    backs[0].start()
    backs[1].start()
    grams.finish()
    backs[0].scatter()
    backs[1].scatter()
    gram[0:256, 0:256] = gfull[0:256]
    gram[0:256, 256:512] = gfull[256:512]
    gram[256:512, 256:512] = gfull[512:768]

    def between(k):
        if k == 1:
            backs[0].reduce()
            backs[1].reduce()
        if k == 3:
            backs[0].forward()
            backs[1].forward()

    inverse_factor(R1, gram, inv, between)
    h, lo = split(inv[...] * math.sqrt(D))
    vh[...] = h
    vw[...] = lo

    def row_basis(i, carry):
        r = pl.ds(pl.multiple_of(i * 224, 32), 224)
        value = dot3(xh[r, :], xw[r, :], vh[...], vw[...], 1, 1)
        rb[r, :] = value
        h, lo = split(value)
        xh[r, :] = h
        xw[r, :] = lo
        return carry

    lax.fori_loop(0, 4, row_basis, 0)
    rb_store = pltpu.make_async_copy(rb, rb_hbm, local_sem.at[10])
    rb_store.start()
    backs[0].finish()
    backs[1].finish()

    def core_two(i, carry):
        r = pl.ds(pl.multiple_of(i * 256, 256), 256)
        h, lo = split(jnp.concatenate([cfull[0, r, :], cfull[1, r, :]], axis=1))
        h, lo = split(dot3(h, lo, vh[...], vw[...], 1, 1))
        th[r, :] = h
        tw[r, :] = lo
        return carry

    lax.fori_loop(0, 4, core_two, 0)

    def back(i, carry):
        r = pl.ds(pl.multiple_of(i * 256, 256), 256)
        pth[r, :] = dot3(th[r, :], tw[r, :], xh[...], xw[...], 1, 1).astype(BF16)
        return carry

    lax.fori_loop(0, 4, back, 0)

    def column_image(i, carry, half):
        f = pl.multiple_of(half * 1024 + i * 256, 256)
        value = dot(pth[0:256, :], w[0, :, pl.ds(f, 256)], 1, 0)
        for e in range(1, 4):
            value = value + dot(pth[256 * e : 256 * e + 256, :], w[e, :, pl.ds(f, 256)], 1, 0)
        s = half * 8 + i * 2
        dp[s] = value[:, :128]
        dp[s + 1] = value[:, 128:]
        return carry

    lax.fori_loop(0, 4, functools.partial(column_image, half=1 - c), 0)
    swap = sender.copy(dp.at[pl.ds((1 - c) * 8, 8)], dsib, "c", 1)
    swap.start()
    lax.fori_loop(0, 4, functools.partial(column_image, half=c), 0)
    groups = [("zxy", 0, 3), ("xyz", 3, 3), ("yzx", 6, 2)]
    cubes = [
        CubeSum(sender, axes, u0, n, dp, darr1, dsum1, darr2, dsum2, darr3, df)
        for axes, u0, n in groups
    ]
    swap.wait()
    for one, (axes, u0, n) in zip(cubes, groups):
        mine = pl.ds(c * 8 + u0, n)
        dp[mine] = dp[mine] + dsib[pl.ds(u0, n)]
        one.start()
    for step in ("reduce1", "reduce2", "reduce3", "gather", "across", "finish"):
        for one in cubes:
            getattr(one, step)()

    for s in range(16):
        h, lo = split(df[s])
        if s == 0:
            value = dot3(h, lo, h, lo, 1, 1)
        else:
            value = value + dot3(h, lo, h, lo, 1, 1)
    gram[0:256, 0:256] = value
    inverse_factor(R2, gram.at[0:256, 0:256], inv.at[0:256, 0:256])
    h, lo = split(inv[0:256, 0:256] * math.sqrt(F))
    vh[0:256, 0:256] = h
    vw[0:256, 0:256] = lo
    stores = []
    for s in range(16):
        h, lo = split(df[s].T)
        value = dot3(h, lo, vh[0:256, 0:256], vw[0:256, 0:256], 1, 1)
        dp[s // 2, 128 * (s % 2) : 128 * (s % 2) + 128] = value[:, :128]
        dp[8 + s // 2, 128 * (s % 2) : 128 * (s % 2) + 128] = value[:, 128:]
        if s % 2:
            t = s // 2
            for g in range(2):
                store = pltpu.make_async_copy(
                    dp.at[8 * g + t],
                    cb_hbm.at[pl.ds(256 * t, 256), pl.ds(128 * g, 128)],
                    local_sem.at[11 + 2 * t + g],
                )
                store.start()
                stores.append(store)
    for store in stores:
        store.wait()
    rb_store.wait()


COPIES = 160


def shards(weights, prev_rows, prev_cols):
    vm = pltpu.VMEM
    return pl.pallas_call(
        kernel,
        name="orthogonal_step",
        out_shape=(
            jax.ShapeDtypeStruct((ROWS, R1), F32),
            jax.ShapeDtypeStruct((F, R2), F32),
        ),
        in_specs=[pl.BlockSpec(memory_space=pl.ANY)] * 3,
        out_specs=[pl.BlockSpec(memory_space=pl.ANY)] * 2,
        scratch_shapes=[
            vm((LOCAL, ROWS, F), BF16),
            vm((ROWS, 1024), BF16), vm((ROWS, 1024), BF16),
            vm((1024, ROWS), BF16), vm((1024, ROWS), BF16),
            vm((ROWS, R1), BF16), vm((ROWS, R1), BF16),
            vm((F, R2), BF16), vm((ROWS, R2), F32),
            vm((2, 1024, 256), F32), vm((2, 512, 256), F32), vm((2, 3, 128, 256), F32),
            vm((2, 1024, 256), F32), vm((1024, 256), BF16), vm((1024, 256), BF16),
            vm((4, ROWS, 128), F32), vm((4, 3, 224, 128), F32), vm((4, 224, 128), F32),
            vm((4, 3, 56, 128), F32), vm((4, ROWS, 128), F32),
            vm((768, 256), F32), vm((384, 256), F32), vm((3, 96, 256), F32), vm((768, 256), F32),
            vm((R1, R1), F32), vm((R1, R1), F32), vm((R1, R1), BF16), vm((R1, R1), BF16),
            vm((1024, R1), BF16), vm((1024, R1), BF16),
            vm((ROWS, R1), F32),
            vm((16, 256, 128), F32), vm((8, 256, 128), F32), vm((3, 8, 64, 128), F32),
            vm((8, 64, 128), F32), vm((3, 8, 16, 128), F32), vm((8, 16, 128), F32),
            vm((4, 8, 16, 128), F32), vm((16, 256, 128), F32),
            pltpu.SemaphoreType.DMA((32,)),
            pltpu.SemaphoreType.DMA((COPIES,)),
            pltpu.SemaphoreType.DMA((COPIES,)),
        ],
        compiler_params=pltpu.CompilerParams(
            collective_id=0, has_side_effects=True, vmem_limit_bytes=62 * 2**20
        ),
        cost_estimate=pl.CostEstimate(flops=12 * 10**9, bytes_accessed=25 * 10**6, transcendentals=0),
    )(weights, prev_rows, prev_cols)


def solution(mesh):
    placed = (P("expert", "row", None), P("row", None), P())
    return jax.shard_map(
        shards, mesh=mesh, in_specs=placed, out_specs=(P("row", None), P()), check_vma=False
    )
```

time: 756 us -> 181 us (0.24); the launches traced: 748 us -> 181 us
  waiting for transfers between devices: 429 us -> 0 us
  other arithmetic: 180 us -> 0 us
  Pallas kernels: 0 us -> 176 us
  matrix products: 89 us -> 0 us
  local copies, waits for them, and re-layouts: 30.2 us -> 4.34 us
  between operations: 18.4 us -> 0.65 us
    psum x5 -> x0, waiting for transfers between devices: 429 us -> none  [the longest x1 146 us: shards(): colimg = lax.psum(terms, ('expert', 'row'))]
    pallas_call x0 -> x1, Pallas kernels: none -> 176 us  [shards(): pl.pallas_call(kernel, name='orthogonal_step', out_shape=(jax.ShapeDtypeS...]
    another operation x27 -> x0, other arithmetic: 175 us -> none  [the longest x21 113 us: orthogonal_part(): factor = jnp.linalg.cholesky(gram)]
    dot_general x8 -> x0, matrix products: 66.9 us -> none  [the longest x1 13.4 us: cores_under(): jnp.einsum('rj,erk->ejk', row_basis, proj, precision=lax.Precision.HIGHEST)]
    another operation x18 -> x0, matrix products: 22.1 us -> none  [the longest x10 16.2 us: orthogonal_part(): jax.scipy.linalg.solve_triangular(factor, images.T, lower=True)]
    another operation x26 -> x0, local copies, waits for them, and re-layouts: 18.1 us -> none
  transfers between devices with their start and end apart: 5 -> 0, of which waited for: 5 -> 0; matrix products, arithmetic and copies ran while one was open for 1% -> 0% of each run, Pallas kernels for 0% -> 0%
where the time goes in v1:
time: 181 us
  Pallas kernels  176 us (97%)
  local copies, waits for them, and re-layouts  4.34 us (2%)
    pallas_call x1, Pallas kernels, shards(): pl.pallas_call(kernel, name='orthogonal_step', out_shape=(jax.ShapeDtypeS...  176 us
    unnamed x4, local copies, waits for them, and re-layouts  4.34 us

profile of v1, /device:TPU:1, one launch (start us, length us, event | category | flops | bytes accessed | tf_op | source)
XLA Modules:
  0.0 180.7 jit_solution(6954702069757789276)
XLA Ops:
  0.6 175.7 %orthogonal_step.1 = (f32[896,512]{1,0:T(8,128)}, f32[2048,256]{1,0:T(8,128)}) custom-call(bf16[4,896,2048]{2,1,0:T(8,128)(2,1)} %w_hbm.1, f32[896,512]{1,0:T(8,128)} %x_hbm.1, f32[2048,256]{1,0:T(8,128)} %c_hbm.1), custom_call_target="tpu_custom_call" | custom-call | flops 12000000000 | bytes 25000000 | tf_op jit(solution)/shard_map/orthogonal_step/pallas_call | solution.py:621
  176.4 0.0 copy-start
  176.4 3.0 %copy.7 = f32[896,512]{1,0:T(8,128)} copy(f32[896,512]{1,0:T(8,128)} %get-tuple-element.4) | data formatting | bytes 3670016
  179.4 0.0 copy-done
  179.4 1.3 copy.8
Async XLA Ops:
  176.4 3.0 %copy-start = (f32[2048,256]{1,0:T(8,128)S(1)}, f32[2048,256]{1,0:T(8,128)}, u32[]{:S(2)}) copy-start(f32[2048,256]{1,0:T(8,128)} %get-tuple-element.5) | copy-start | bytes 6291460
